TPU v7x, 128 devices: a whole 4x4x4 slice. The times are simulated.
128 devices in a mesh: node: 32 (over z, y, core), local: 4 (over x).
Axes of the slice: x: 4, y: 4, z: 4, core: 2. Of those that a mesh axis runs over, the one named last changes fastest.
Arguments:
- tokens: bfloat16 [16384, 7168], P(('node', 'local')), may hold values from -6 to 6
- node_set: int32 [16384, 2], P(('node', 'local')), may hold values from 0 to 31, all different within a row; in each aligned block of 128 rows (0 to 127, 128 to 255, ...) at most 12 rows name the same one
- gate_weights: float32 [16384, 2], P(('node', 'local')), may hold values from 0.2 to 1
- w_gate: bfloat16 [32, 7168, 1024], P('node', 'local'), may hold values from -0.0625 to 0.0625
- w_up: bfloat16 [32, 7168, 1024], P('node', 'local'), may hold values from -0.0625 to 0.0625
- w_down: bfloat16 [32, 1024, 7168], P('node', None, 'local'), may hold values from -0.1875 to 0.1875
Outputs:
- mixed: bfloat16 [16384, 7168], P(('node', 'local'))
Inputs may be any that keep to these rules, and one draw needn't show every extreme that they name: `node_set`: each row names 2 different experts; among the rows of one device no expert is named by more than 12 rows, and in every draw some expert is named by exactly 12 rows of some device.
All inputs are finite; a program needn't handle non-finite values.
Results may differ from a plain program's by a relative error of at most 0.0058.
Values may be sent and summed in bfloat16 or wider, within the bound.
A program may use at most 128 MiB of HBM per device.

v0:
```python
import jax
import jax.numpy as jnp
from jax import lax
from jax.sharding import PartitionSpec as P


def shards(tokens, node_set, gate_weights, w_gate, w_up, w_down):
    node_count = lax.axis_size("node")
    local_count = lax.axis_size("local")
    tok_rows, model_width = tokens.shape
    routes = node_set.shape[1]
    quarter = model_width // local_count
    capacity = 3 * tok_rows * routes // (2 * node_count)
    member = (
        node_set[:, :, None] == jnp.arange(node_count, dtype=jnp.int32)[None, None, :]
    ).astype(jnp.int32)
    counts = jnp.sum(member, axis=1)
    slot_of = jnp.cumsum(counts, axis=0) - counts
    route_slot = jnp.sum(member * slot_of[:, None, :], axis=2)
    slot_match = (counts[:, :, None] == 1) & (
        slot_of[:, :, None] == jnp.arange(capacity, dtype=jnp.int32)[None, None, :]
    )
    positions = jnp.arange(tok_rows, dtype=jnp.int32)
    source_row = jnp.sum(slot_match.astype(jnp.int32) * positions[:, None, None], axis=0)
    filled = jnp.any(slot_match, axis=0)
    picked = jnp.take(tokens, source_row.reshape(-1), axis=0).reshape(
        node_count, capacity, model_width
    )
    picked = jnp.where(filled[:, :, None], picked, jnp.zeros((), tokens.dtype))
    outgoing = picked.reshape(node_count, capacity, local_count, quarter)
    flat_send = outgoing.transpose(0, 2, 1, 3).reshape(node_count * local_count, capacity, quarter)
    arrived = lax.all_to_all(flat_send, ("node", "local"), split_axis=0, concat_axis=0, tiled=True)
    shape_in = arrived.shape
    flat_rows = arrived.reshape(-1, quarter)
    gate_mat = w_gate[0]
    up_mat = w_up[0]
    down_mat = w_down[0]
    pre_gate = jnp.dot(flat_rows, gate_mat, preferred_element_type=jnp.float32)
    pre_up = jnp.dot(flat_rows, up_mat, preferred_element_type=jnp.float32)
    sum_gate, sum_up = lax.psum((pre_gate, pre_up), "local")
    hidden = (jax.nn.silu(sum_gate) * sum_up).astype(jnp.bfloat16)
    result = (
        jnp.dot(hidden, down_mat, preferred_element_type=jnp.float32)
        .astype(jnp.bfloat16)
        .reshape(shape_in)
    )
    returned = lax.all_to_all(result, ("node", "local"), split_axis=0, concat_axis=0, tiled=True)
    returned = returned.reshape(node_count, local_count, capacity, quarter).transpose(0, 2, 1, 3)
    answers = returned.reshape(node_count * capacity, model_width)
    flat_index = (node_set * capacity + route_slot).reshape(-1)
    gathered = jnp.take(answers, flat_index, axis=0).reshape(tok_rows, routes, model_width)
    mixed = jnp.zeros((tok_rows, model_width), jnp.float32)
    for route in range(routes):
        mixed = mixed + gate_weights[:, route][:, None] * gathered[:, route].astype(jnp.float32)
    return mixed.astype(jnp.bfloat16)


def solution(mesh):
    placed = (
        P(("node", "local"), None),
        P(("node", "local"), None),
        P(("node", "local"), None),
        P("node", "local", None),
        P("node", "local", None),
        P("node", None, "local"),
    )
    return jax.shard_map(
        shards, mesh=mesh, in_specs=placed, out_specs=P(("node", "local"), None), check_vma=False
    )
```

profile of v0, /device:TPU:1, one launch (start us, length us, event | category | flops | bytes accessed | tf_op | source)
XLA Modules:
  0.0 553.0 jit_solution(17321824543014493089)
XLA Ops:
  6.5 0.0 copy-start
  6.5 0.0 all-reduce.3.cloned.1.call-start
  6.5 0.8 convert_reduce_fusion
  7.4 0.1 copy.14
  7.5 0.2 reduce_window_sum.11
  7.7 0.1 copy.16
  7.7 0.3 fusion.9
  8.0 0.3 select_reduce_fusion
  8.3 0.1 copy.20
  8.4 0.1 copy.19
  8.5 0.1 copy.18
  8.6 0.1 reshape.122
  8.8 0.0 copy-done
  8.8 6.5 %gather_fusion = bf16[384,7168]{1,0:T(8,128)(2,1)} fusion(bf16[128,7168]{1,0:T(8,128)(2,1)S(1)} %copy-done, s32[1024]{0:T(1024)S(1)} %pad_clamp_fusion.1), kind=kCustom, calls=%fused_computation | custom fusion | bytes 11011584 | tf_op jit(solution)/shard_map/jit(_take)/gather | solution.py:26
  15.2 8.0 %gather.13 = bf16[32,12,7168]{2,1,0:T(8,128)(2,1)} reshape(bf16[384,7168]{1,0:T(8,128)(2,1)} %gather_fusion) | data formatting | bytes 11010048 | tf_op jit(solution)/shard_map/jit(_take)/gather | solution.py:26
  23.3 4.0 select_select_fusion
  27.3 0.5 fusion.12
  27.8 4.1 pad_maximum_fusion
  31.9 9.3 %reshape.123 = bf16[128,12,1792]{2,1,0:T(8,128)(2,1)} reshape(bf16[32,48,1792]{2,1,0:T(8,128)(2,1)} %pad_maximum_fusion) | data formatting | bytes 11010048 | tf_op jit(solution)/shard_map/reshape | solution.py:31
  41.2 98.9 %all_to_all.10 = bf16[128,12,1792]{2,1,0:T(8,128)(2,1)} all-to-all(bf16[128,12,1792]{2,1,0:T(8,128)(2,1)} %reshape.123), channel_id=1, replica_groups=mesh['node'=32,'local'=4] {'node','local'}, dimensions={0} | all-to-all | bytes 11010048 | tf_op jit(solution)/shard_map/all_to_all | solution.py:32
  140.1 9.4 %reshape.124 = bf16[1536,1792]{1,0:T(8,128)(2,1)} reshape(bf16[128,12,1792]{2,1,0:T(8,128)(2,1)} %all_to_all.10) | data formatting | bytes 11010048 | tf_op jit(solution)/shard_map/reshape | solution.py:34
  149.4 0.0 copy-start.2
  149.4 0.0 copy-start.5
  149.4 10.7 %fusion.3 = f32[1536,1024]{1,0:T(8,128)} fusion(bf16[1536,1792]{1,0:T(8,128)(2,1)} %reshape.124, bf16[1,1792,1024]{2,1,0:T(8,128)(2,1)} %param.10), kind=kOutput, calls=%fused_computation.11 | convolution fusion | flops 5637144576 | bytes 15466496 | tf_op jit(solution)/shard_map/dot_general | solution.py:39
  160.1 0.0 copy-done.2
  160.1 0.0 copy-done.5
  160.1 7.7 %fusion.5 = f32[1536,1024]{1,0:T(8,128)} fusion(bf16[1536,1792]{1,0:T(8,128)(2,1)S(1)} %copy-done.2, bf16[1,1792,1024]{2,1,0:T(8,128)(2,1)S(1)} %copy-done.5), kind=kOutput, calls=%fused_computation.13 | convolution fusion | flops 5637144576 | bytes 15466496 | tf_op jit(solution)/shard_map/dot_general | solution.py:38
  167.8 0.0 all-reduce.3.cloned.1.call-update
  167.8 223.3 %all-reduce.3.cloned.1.call-done = (f32[1536,1024]{1,0:T(8,128)}, f32[1536,1024]{1,0:T(8,128)}) async-done(((f32[1536,1024]{1,0:T(8,128)}, f32[1536,1024]{1,0:T(8,128)}), (f32[1536,1024]{1,0:T(8,128)}, f32[1536,1024]{1,0:T(8,128)})) %all-reduce.3.cloned.1.call-update) | async-done | bytes 12582928 | tf_op jit(solution)/shard_map/psum | solution.py:40
  391.2 12.3 %convolution_convert_fusion = bf16[1536,1792]{1,0:T(8,128)(2,1)} fusion(bf16[1,1024,1792]{2,1,0:T(8,128)(2,1)} %param.11, f32[1536,1024]{1,0:T(8,128)} %get-tuple-element.5, f32[1536,1024]{1,0:T(8,128)} %get-tuple-element.6), kind=kOutput, calls=%fused_computation.2 | convolution fusion | flops 5649334272 | bytes 21757952 | tf_op jit(solution)/shard_map/dot_general | solution.py:43
  403.5 9.3 %reshape.125 = bf16[128,12,1792]{2,1,0:T(8,128)(2,1)} reshape(bf16[1536,1792]{1,0:T(8,128)(2,1)} %convolution_convert_fusion) | data formatting | bytes 11010048 | tf_op jit(solution)/shard_map/reshape | solution.py:45
  412.7 0.0 copy-start.3
  412.7 0.0 copy-start.4
  412.7 8.7 %all-to-all-start.1 = ((bf16[128,12,1792]{2,1,0:T(8,128)(2,1)}), bf16[128,12,1792]{2,1,0:T(8,128)(2,1)}, u32[]{:S(2)}, u32[]{:S(2)}) async-start(bf16[128,12,1792]{2,1,0:T(8,128)(2,1)} %reshape.125), calls=%async_computation.1 | async-start | bytes 14680064 | tf_op jit(solution)/shard_map/all_to_all | solution.py:47
  421.4 0.0 copy-done.3
  421.5 0.1 copy.22
  421.6 0.1 reshape.128
  421.7 0.0 copy-done.4
  421.8 89.9 %all-to-all-done.1 = bf16[128,12,1792]{2,1,0:T(8,128)(2,1)} async-done(((bf16[128,12,1792]{2,1,0:T(8,128)(2,1)}), bf16[128,12,1792]{2,1,0:T(8,128)(2,1)}, u32[]{:S(2)}, u32[]{:S(2)}) %all-to-all-start.1) | async-done | bytes 5505056 | tf_op jit(solution)/shard_map/all_to_all | solution.py:47
  511.7 5.9 %copy.21 = bf16[32,4,12,1792]{3,1,2,0:T(4,128)(2,1)S(1)} copy(bf16[32,4,12,1792]{3,2,1,0:T(8,128)(2,1)} %bitcast.4) | data formatting | bytes 11010048 | tf_op jit(solution)/shard_map/reshape | solution.py:48
  517.6 3.5 copy.24
  521.1 11.3 %gather_fusion.1 = bf16[256,7168]{1,0:T(8,128)(2,1)} fusion(bf16[384,7168]{1,0:T(8,128)(2,1)} %bitcast.31, s32[1024]{0:T(1024)S(1)} %pad_clamp_fusion), kind=kCustom, calls=%fused_computation.1 | custom fusion | bytes 7341056 | tf_op jit(solution)/shard_map/jit(_take)/gather | solution.py:51
  532.4 8.1 %gather.15 = bf16[128,2,7168]{2,1,0:T(2,128)(2,1)} reshape(bf16[256,7168]{1,0:T(8,128)(2,1)} %gather_fusion.1) | data formatting | bytes 7340032 | tf_op jit(solution)/shard_map/jit(_take)/gather | solution.py:51
  540.6 0.0 copy-start.1
  540.6 3.6 copy_select_fusion
  544.2 2.0 fusion.1
  546.2 0.0 copy-done.1
  (10 shorter events, 0.1 us)
Async XLA Ops:
  6.5 2.2 copy-start
  6.5 384.6 %all-reduce.3.cloned.1.call-start = ((), (), s32[]{:S(2)}) async-start(), calls=%async_computation.2 | async-start | bytes 25165824 | tf_op jit(solution)/shard_map/psum | solution.py:40
  149.4 10.7 %copy-start.2 = (bf16[1536,1792]{1,0:T(8,128)(2,1)S(1)}, bf16[1536,1792]{1,0:T(8,128)(2,1)}, u32[]{:S(2)}) copy-start(bf16[1536,1792]{1,0:T(8,128)(2,1)} %reshape.124) | copy-start | bytes 16515076
  149.4 10.7 %copy-start.5 = (bf16[1,1792,1024]{2,1,0:T(8,128)(2,1)S(1)}, bf16[1,1792,1024]{2,1,0:T(8,128)(2,1)}, u32[]{:S(2)}) copy-start(bf16[1,1792,1024]{2,1,0:T(8,128)(2,1)} %param.9) | copy-start | bytes 11010052
  412.7 8.7 %copy-start.3 = (s32[128,2]{0,1:T(2,128)S(1)}, s32[128,2]{0,1:T(2,128)}, u32[]{:S(2)}) copy-start(s32[128,2]{0,1:T(2,128)} %param.7) | copy-start | bytes 3076
  412.7 9.0 %copy-start.4 = (f32[128,2]{0,1:T(2,128)S(1)}, f32[128,2]{0,1:T(2,128)}, u32[]{:S(2)}) copy-start(f32[128,2]{0,1:T(2,128)} %param.8) | copy-start | bytes 3076
  412.7 98.9 %all-to-all-start.1 = ((bf16[128,12,1792]{2,1,0:T(8,128)(2,1)}), bf16[128,12,1792]{2,1,0:T(8,128)(2,1)}, u32[]{:S(2)}, u32[]{:S(2)}) async-start(bf16[128,12,1792]{2,1,0:T(8,128)(2,1)} %reshape.125), calls=%async_computation.1 | async-start | bytes 14680064 | tf_op jit(solution)/shard_map/all_to_all | solution.py:47
  540.6 5.6 %copy-start.1 = (bf16[128,7168]{1,0:T(8,128)(2,1)S(1)}, bf16[128,7168]{1,0:T(8,128)(2,1)}, u32[]{:S(2)}) copy-start(bf16[128,7168]{1,0:T(8,128)(2,1)} %param.6) | copy-start | bytes 5505028
Sparse Core Ops, SparseCore 0:
  167.9 223.1 all-reduce.2
where the time goes:
time: 554 us; the launch traced here: 553 us
  waiting for transfers between devices  313 us (56%)
  blocking collectives  98.9 us (18%)
  local copies, waits for them, and re-layouts  72.6 us (13%)
  matrix products  30.7 us (6%)
  other arithmetic  15.4 us (3%)
  between operations  13.5 us (2%)
  starting transfers between devices  8.69 us (2%)
    psum x1, waiting for transfers between devices, shards(): sum_gate, sum_up = lax.psum((pre_gate, pre_up), 'local')  223 us
    all_to_all x1, blocking collectives, shards(): lax.all_to_all(flat_send, ('node', 'local'), split_axis=0, concat_axis=0,...  98.9 us
    all_to_all x1, waiting for transfers between devices, shards(): lax.all_to_all(result, ('node', 'local'), split_axis=0, concat_axis=0, ti...  89.9 us
    gather x2, local copies, waits for them, and re-layouts, shards(): jnp.take(answers, flat_index, axis=0).reshape(tok_rows, routes, model_width)  19.5 us
    gather x2, local copies, waits for them, and re-layouts, shards(): jnp.take(tokens, source_row.reshape(-1), axis=0)  14.5 us
    dot_general x1, matrix products, shards(): jnp.dot(hidden, down_mat, preferred_element_type=jnp.float32)  12.3 us
  transfers between devices with their start and end apart: 2, of which 2 were waited for; matrix products, arithmetic and copies ran while one was open for 0% of the time, Pallas kernels for 0%

commit v1 on v0

v1 whole, which is shorter than its diff:
```python
import functools

import jax
import jax.numpy as jnp
from jax import lax
from jax.experimental import pallas as pl
from jax.experimental.pallas import tpu as pltpu
from jax.sharding import PartitionSpec as P

MESH = pl.DeviceIdType.MESH
F32 = jnp.float32
BF16 = jnp.bfloat16
CHIPS = (
    (0, 0), (1, 0), (3, 0), (0, 2),
    (3, 3), (1, 3), (3, 1), (2, 1),
    (1, 2), (3, 2), (2, 3), (2, 2),
    (0, 1), (0, 3), (2, 0), (1, 1),
)
OFFSETS = tuple((dz, dy, dc) for dz, dy in CHIPS for dc in range(2))
NODES, LOCALS = 32, 4
GROUPS = 4
PER = NODES // GROUPS


def kernel(tok_rows, quarter, ff, cap,
           meta_ref, tok_ref, wg_ref, wu_ref, wd_ref, out_ref,
           meta, xin, pick, sbuf, abuf, wgu, wd, pre, rsbuf, hid, rbuf, uhi, ulo, acc, mbuf,
           w_sem, l_sem, ms_sem, mr_sem, xs_sem, xr_sem, ds_sem, dr_sem, ps_sem, pr_sem, hs_sem, hr_sem,
           as_sem, ar_sem, fs_sem, fr_sem):
    slots = LOCALS * cap
    grows = PER * slots
    own = grows // LOCALS
    node, loc = lax.axis_index("node"), lax.axis_index("local")
    z, y, c = node // 8, (node // 2) % 4, node % 2

    def to(o):
        dz, dy, dc = OFFSETS[o]
        return (((z + dz) % 4) * 4 + (y + dy) % 4) * 2 + (c + dc) % 2

    def back(o):
        dz, dy, dc = OFFSETS[o]
        return (((z + 4 - dz) % 4) * 4 + (y + 4 - dy) % 4) * 2 + (c + dc) % 2

    def xto(d):
        return (loc + d) % LOCALS

    barrier = pltpu.get_barrier_semaphore()
    for o in range(1, NODES):
        pl.semaphore_signal(barrier, inc=1, device_id=(to(o), loc), device_id_type=MESH)
    for d in range(1, LOCALS):
        pl.semaphore_signal(barrier, inc=1, device_id=(node, xto(d)), device_id_type=MESH)

    def rows(ref, start, size):
        return ref.at[pl.ds(pl.multiple_of(start, 16), size)]

    def cols(j):
        return pl.ds(pl.multiple_of(j * quarter, 128), quarter)

    w_copies = [
        pltpu.make_async_copy(wg_ref.at[0], wgu.at[:, pl.ds(0, ff)], w_sem.at[0]),
        pltpu.make_async_copy(wu_ref.at[0], wgu.at[:, pl.ds(ff, ff)], w_sem.at[1]),
        pltpu.make_async_copy(wd_ref.at[0], wd, w_sem.at[2]),
    ]
    own_tok = pltpu.make_async_copy(tok_ref.at[:, cols(loc)], rows(xin, loc * tok_rows, tok_rows), l_sem.at[0])
    own_tok.start()
    pl.semaphore_wait(barrier, NODES - 1 + LOCALS - 1)

    def remote(src, dst, ss, rs, n, x):
        return pltpu.make_async_remote_copy(
            src_ref=src, dst_ref=dst, send_sem=ss, recv_sem=rs, device_id=(n, x), device_id_type=MESH)

    meta_copies, x_copies = [], []
    for d in (2, 1, 3):
        meta_copies.append(remote(meta_ref, meta.at[loc], ms_sem.at[d - 1], mr_sem.at[d - 1], node, xto(d)))
        meta_copies[-1].start()
    for d in (2, 1, 3):
        x_copies.append(remote(tok_ref.at[:, cols(xto(d))], rows(xin, loc * tok_rows, tok_rows),
                               xs_sem.at[d - 1], xr_sem.at[d - 1], node, xto(d)))
        x_copies[-1].start()
    for w in w_copies:
        w.start()
    meta[loc] = meta_ref[...]
    own_tok.wait()
    for m in meta_copies:
        m.wait()
    for m in x_copies:
        m.wait()

    d_copies = []
    for g in range(GROUPS):
        at = lax.broadcasted_iota(jnp.int32, (slots, tok_rows), 0)
        for i in range(PER):
            row_id = (at + to(g * PER + i) * slots).astype(F32)
            for b in range(LOCALS):
                d0 = meta[b, 0:1, :] + float(b * cap)
                d1 = meta[b, 1:2, :] + float(b * cap)
                hit = jnp.where(row_id == d0, 1.0, 0.0) + jnp.where(row_id == d1, 1.0, 0.0)
                pick[i * slots:(i + 1) * slots, b * tok_rows:(b + 1) * tok_rows] = hit.astype(BF16)

        @pl.loop(0, quarter // 256)
        def _(t):
            at = pl.ds(pl.multiple_of(t * 256, 256), 256)
            sbuf[g * grows:(g + 1) * grows, at] = jnp.dot(
                pick[...], xin[:, at], preferred_element_type=F32).astype(BF16)

        for o in range(g * PER, (g + 1) * PER):
            src, dst = sbuf.at[pl.ds(o * slots, slots)], abuf.at[pl.ds(o * slots, slots)]
            if o == 0:
                d_copies.append(pltpu.make_async_copy(src, dst, l_sem.at[1]))
            else:
                d_copies.append(remote(src, dst, ds_sem.at[o], dr_sem.at[o], to(o), loc))
            d_copies[-1].start()

    p_copies, h_copies, a_copies = {}, {}, {}

    def stage_a(g):
        for o in range(g * PER, (g + 1) * PER):
            d_copies[o].wait() if o == 0 else d_copies[o].wait_recv()
        if g == 0:
            w_copies[0].wait()
            w_copies[1].wait()

        @pl.loop(0, 2 * ff // 256)
        def _(t):
            at = pl.ds(pl.multiple_of(t * 256, 256), 256)
            pre[g * grows:(g + 1) * grows, at] = jnp.dot(
                abuf[g * grows:(g + 1) * grows, :], wgu[:, at], preferred_element_type=F32).astype(BF16)

        for d in (2, 1, 3):
            p_copies[g, d] = remote(rows(pre, g * grows + xto(d) * own, own), rsbuf.at[g, d - 1],
                                    ps_sem.at[g, d - 1], pr_sem.at[g, d - 1], node, xto(d))
            p_copies[g, d].start()

    def stage_b(g):
        for d in (2, 1, 3):
            p_copies[g, d].wait_recv()
        mine = pl.ds(pl.multiple_of(g * grows + loc * own, 16), own)

        @pl.loop(0, ff // 256)
        def _(t):
            at_g = pl.ds(pl.multiple_of(t * 256, 256), 256)
            at_u = pl.ds(pl.multiple_of(t * 256 + ff, 256), 256)
            gate, up = pre[mine, at_g].astype(F32), pre[mine, at_u].astype(F32)
            for d in range(3):
                gate = gate + rsbuf[g, d, :, at_g].astype(F32)
                up = up + rsbuf[g, d, :, at_u].astype(F32)
            hid[mine, at_g] = (gate / (1.0 + jnp.exp(-gate)) * up).astype(BF16)

        for d in (2, 1, 3):
            h_copies[g, d] = remote(hid.at[mine], hid.at[mine], hs_sem.at[g, d - 1], hr_sem.at[g, d - 1],
                                    node, xto(d))
            h_copies[g, d].start()

    def stage_c(g):
        for d in (2, 1, 3):
            h_copies[g, d].wait_recv()
        if g == 0:
            w_copies[2].wait()

        @pl.loop(0, quarter // 256)
        def _(t):
            at = pl.ds(pl.multiple_of(t * 256, 256), 256)
            abuf[g * grows:(g + 1) * grows, at] = jnp.dot(
                hid[g * grows:(g + 1) * grows, :], wd[:, at], preferred_element_type=F32).astype(BF16)

        for o in range(g * PER, (g + 1) * PER):
            src, dst = abuf.at[pl.ds(o * slots, slots)], rbuf.at[pl.ds(o * slots, slots)]
            if o == 0:
                a_copies[o] = pltpu.make_async_copy(src, dst, l_sem.at[2])
            else:
                a_copies[o] = remote(src, dst, as_sem.at[o], ar_sem.at[o], back(o), loc)
            a_copies[o].start()

    def mix_weights(g):
        spot = lax.broadcasted_iota(jnp.int32, (tok_rows, grows), 1)
        slot_id = spot + (to(g * PER) - 0) * slots
        for i in range(1, PER):
            slot_id = jnp.where(spot >= i * slots, spot + (to(g * PER + i) - i) * slots, slot_id)
        slot_id = slot_id.astype(F32)
        for b in range(LOCALS):
            m = jnp.transpose(meta[b])
            d0, d1 = m[:, 0:1] + float(b * cap), m[:, 1:2] + float(b * cap)
            w = jnp.where(slot_id == d0, m[:, 2:3], 0.0) + jnp.where(slot_id == d1, m[:, 3:4], 0.0)
            high = w.astype(BF16)
            uhi[b * tok_rows:(b + 1) * tok_rows, :] = high
            ulo[b * tok_rows:(b + 1) * tok_rows, :] = (w - high.astype(F32)).astype(BF16)

    def stage_m(g):
        mix_weights(g)
        for o in range(g * PER, (g + 1) * PER):
            a_copies[o].wait() if o == 0 else a_copies[o].wait_recv()

        @pl.loop(0, quarter // 256)
        def _(t):
            at = pl.ds(pl.multiple_of(t * 256, 256), 256)
            got = rbuf[g * grows:(g + 1) * grows, at]
            part = jnp.dot(uhi[...], got, preferred_element_type=F32) + jnp.dot(
                ulo[...], got, preferred_element_type=F32)
            if g > 0:
                part = part + acc[:, at]
            if g < GROUPS - 1:
                acc[:, at] = part
            else:
                mbuf[:, at] = part.astype(BF16)

    for step in range(GROUPS + 2):
        if step < GROUPS:
            stage_a(step)
        if 1 <= step <= GROUPS:
            stage_b(step - 1)
        if step >= 2:
            stage_c(step - 2)
    for g in range(GROUPS):
        stage_m(g)

    f_copies = []
    for d in (2, 1, 3):
        f_copies.append(remote(rows(mbuf, xto(d) * tok_rows, tok_rows), out_ref.at[:, cols(loc)],
                               fs_sem.at[d - 1], fr_sem.at[d - 1], node, xto(d)))
        f_copies[-1].start()
    own_out = pltpu.make_async_copy(rows(mbuf, loc * tok_rows, tok_rows), out_ref.at[:, cols(loc)], l_sem.at[3])
    own_out.start()
    for o in range(1, NODES):
        d_copies[o].wait_send()
        a_copies[o].wait_send()
    for g in range(GROUPS):
        for d in (1, 2, 3):
            p_copies[g, d].wait_send()
            h_copies[g, d].wait_send()
    own_out.wait()
    for f in f_copies:
        f.wait()


def shards(tokens, node_set, gate_weights, w_gate, w_up, w_down):
    tok_rows, width = tokens.shape
    quarter = width // LOCALS
    ff = w_gate.shape[2]
    routes = node_set.shape[1]
    cap = 3 * tok_rows * routes // (2 * NODES)
    slots = LOCALS * cap
    total = NODES * slots
    grows = total // GROUPS
    own = grows // LOCALS

    member = node_set[:, :, None] == jnp.arange(NODES, dtype=jnp.int32)[None, None, :]
    counts = jnp.sum(member.astype(F32), axis=1)
    earlier = jnp.tri(tok_rows, k=-1, dtype=BF16)
    before = jnp.dot(earlier, counts.astype(BF16), preferred_element_type=F32)
    slot = jnp.sum(jnp.where(member, before[:, None, :], 0.0), axis=2)
    dest = (node_set * slots).astype(F32) + slot
    meta = jnp.concatenate([dest.T, gate_weights.T, jnp.zeros((4, tok_rows), F32)], axis=0)

    any_spec = pl.BlockSpec(memory_space=pl.ANY)
    dma = pltpu.SemaphoreType.DMA
    return pl.pallas_call(
        functools.partial(kernel, tok_rows, quarter, ff, cap),
        name="routed_experts",
        out_shape=jax.ShapeDtypeStruct((tok_rows, width), BF16),
        in_specs=[pl.BlockSpec(memory_space=pltpu.VMEM)] + [any_spec] * 4,
        out_specs=any_spec,
        scratch_shapes=[
            pltpu.VMEM((LOCALS, 8, tok_rows), F32),
            pltpu.VMEM((LOCALS * tok_rows, quarter), BF16),
            pltpu.VMEM((grows, LOCALS * tok_rows), BF16),
            pltpu.VMEM((total, quarter), BF16),
            pltpu.VMEM((total, quarter), BF16),
            pltpu.VMEM((quarter, 2 * ff), BF16),
            pltpu.VMEM((ff, quarter), BF16),
            pltpu.VMEM((total, 2 * ff), BF16),
            pltpu.VMEM((GROUPS, LOCALS - 1, own, 2 * ff), BF16),
            pltpu.VMEM((total, ff), BF16),
            pltpu.VMEM((total, quarter), BF16),
            pltpu.VMEM((LOCALS * tok_rows, grows), BF16),
            pltpu.VMEM((LOCALS * tok_rows, grows), BF16),
            pltpu.VMEM((LOCALS * tok_rows, quarter), F32),
            pltpu.VMEM((LOCALS * tok_rows, quarter), BF16),
            dma((3,)), dma((4,)), dma((3,)), dma((3,)), dma((3,)), dma((3,)),
            dma((NODES,)), dma((NODES,)),
            dma((GROUPS, 3)), dma((GROUPS, 3)), dma((GROUPS, 3)), dma((GROUPS, 3)),
            dma((NODES,)), dma((NODES,)), dma((3,)), dma((3,)),
        ],
        compiler_params=pltpu.CompilerParams(
            collective_id=0, has_side_effects=True, vmem_limit_bytes=60 * 2**20),
        cost_estimate=pl.CostEstimate(flops=20 * 10**9, bytes_accessed=15 * 10**6, transcendentals=10**6),
    )(meta, tokens, w_gate, w_up, w_down)


def solution(mesh):
    placed = (
        P(("node", "local"), None),
        P(("node", "local"), None),
        P(("node", "local"), None),
        P("node", "local", None),
        P("node", "local", None),
        P("node", None, "local"),
    )
    return jax.shard_map(
        shards, mesh=mesh, in_specs=placed, out_specs=P(("node", "local"), None), check_vma=False
    )
```

time: 554 us -> 260 us (0.47)
  the two profiles are of different devices: /device:TPU:1 before, /device:TPU:48 now
where the time goes in v1:
time: 260 us
  Pallas kernels  253 us (97%)
  other arithmetic  3.43 us (1%)
  local copies, waits for them, and re-layouts  2.92 us (1%)
    pallas_call x1, Pallas kernels, shards(): pl.pallas_call(functools.partial(kernel, tok_rows, quarter, ff, cap), nam...  253 us

profile of v1, /device:TPU:48, one launch (start us, length us, event | category | flops | bytes accessed | tf_op | source)
XLA Modules:
  0.0 259.9 jit_solution(10438248155407734150)
XLA Ops:
  0.0 0.1 pad.2.clone
  0.1 0.7 convert_reduce_fusion
  0.8 0.2 fusion
  1.0 0.7 select_reduce_fusion
  1.7 0.7 add_bitcast_fusion
  2.4 1.3 maximum_maximum_fusion.meta_ref
  3.7 253.3 %routed_experts.1 = bf16[128,7168]{1,0:T(8,128)(2,1)} custom-call(f32[8,128]{1,0:T(8,128)} %maximum_maximum_fusion.meta_ref, bf16[128,7168]{1,0:T(8,128)(2,1)} %tok_ref.1, bf16[1,1792,1024]{2,1,0:T(8,128)(2,1)} %wg_ref.1, bf16[1,1792,1024]{2,1,0:T(8,128)(2,1)} %wu_ref.1, bf16[1,1024,1792]{2,1,0:T(8,128)(2,1)} %wd_ref.1), custom_call_target="tpu_custom_call" | custom-call | flops 20000000000 | bytes 15000000 | tf_op jit(solution)/shard_map/routed_experts/pallas_call | solution.py:256
  257.0 2.8 %copy.10 = bf16[128,7168]{1,0:T(8,128)(2,1)} copy(bf16[128,7168]{1,0:T(8,128)(2,1)} %routed_experts.1) | data formatting | bytes 3670016
  (2 shorter events, 0.0 us)

commit v2 on v1

v2 whole, which is shorter than its diff:
```python
import functools

import jax
import jax.numpy as jnp
from jax import lax
from jax.experimental import pallas as pl
from jax.experimental.pallas import tpu as pltpu
from jax.sharding import PartitionSpec as P

MESH = pl.DeviceIdType.MESH
F32 = jnp.float32
BF16 = jnp.bfloat16
NODES, LOCALS = 32, 4
STEPS = ((0, 0), (0, 1), (2, 0), (2, 1), (1, 0), (1, 1), (3, 0), (3, 1))
PLANES = (0, 3, 1, 2)
HALVES = 2
PER = len(STEPS) // HALVES
GROUPS = len(PLANES) * HALVES


def kernel(tok_rows, quarter, ff, cap,
           meta_ref, tok_ref, wg_ref, wu_ref, wd_ref, out_ref,
           meta, zin, pick, sbuf, abuf, wgu, wd, pre, part, ownf, rsbuf, hid, rbuf, uhi, ulo, acc, mbuf,
           w_sem, l_sem, ms_sem, mr_sem, ns_sem, nr_sem, xs_sem, xr_sem, zs_sem, zr_sem, os_sem, or_sem,
           ds_sem, dr_sem, ps_sem, pr_sem, hs_sem, hr_sem, as_sem, ar_sem, fs_sem, fr_sem):
    slots = LOCALS * cap
    prows = len(STEPS) * slots
    grows = PER * slots
    own = grows // LOCALS
    ptok = LOCALS * tok_rows
    node, loc = lax.axis_index("node"), lax.axis_index("local")
    z, y, c = node // 8, (node // 2) % 4, node % 2

    def at_node(dz, dy, dc):
        return (((z + dz) % 4) * 4 + (y + dy) % 4) * 2 + (c + dc) % 2

    def back(r, i):
        dy, dc = STEPS[i]
        return at_node(PLANES[r], 4 - dy, dc)

    def expert(r, i):
        dy, dc = STEPS[i]
        return at_node(4 - PLANES[r], dy, dc)

    def xto(d):
        return (loc + d) % LOCALS

    def rows(ref, start, size):
        return ref.at[pl.ds(pl.multiple_of(start, 16), size)]

    def cols(j):
        return pl.ds(pl.multiple_of(j * quarter, 128), quarter)

    def tile(t, base=0):
        return pl.ds(pl.multiple_of(t * 256 + base, 256), 256)

    def remote(src, dst, ss, rs, n, x):
        return pltpu.make_async_remote_copy(
            src_ref=src, dst_ref=dst, send_sem=ss, recv_sem=rs, device_id=(n, x), device_id_type=MESH)

    barrier = pltpu.get_barrier_semaphore()
    for r in range(len(PLANES)):
        for i in range(len(STEPS)):
            if (r, i) != (0, 0):
                pl.semaphore_signal(barrier, inc=1, device_id=(back(r, i), loc), device_id_type=MESH)
    for d in range(1, LOCALS):
        pl.semaphore_signal(barrier, inc=1, device_id=(node, xto(d)), device_id_type=MESH)
    own_tok = pltpu.make_async_copy(tok_ref.at[:, cols(loc)], rows(zin, loc * tok_rows, tok_rows), l_sem.at[0])
    own_tok.start()
    pl.semaphore_wait(barrier, NODES - 1 + LOCALS - 1)

    m_copies, n_copies, x_copies, z_copies, o_copies = {}, {}, {}, {}, {}
    for d in (1, 3, 2):
        m_copies[d] = remote(meta_ref, meta.at[0, loc], ms_sem.at[d - 1], mr_sem.at[d - 1], node, xto(d))
        m_copies[d].start()

    def z_send(d, src):
        at = ((loc + LOCALS - d) % LOCALS) * tok_rows
        for r, dz in ((1, 1), (2, 3)):
            z_copies[r, d] = remote(src, rows(zin, r * ptok + at, tok_rows), zs_sem.at[r - 1, d], zr_sem.at[r - 1, d],
                                    at_node(dz, 0, 0), loc)
            z_copies[r, d].start()

    def z_forward(d):
        half = tok_rows // 2
        at = ((loc + LOCALS - d) % LOCALS) * tok_rows
        for r, dz, shift in ((1, 1, 0), (2, 3, half)):
            z_copies[r, d].wait_recv()
            o_copies[r, d] = remote(rows(zin, r * ptok + at + shift, half), rows(zin, 3 * ptok + at + shift, half),
                                    os_sem.at[r - 1, d], or_sem.at[r - 1, d], at_node(dz, 0, 0), loc)
            o_copies[r, d].start()

    for d in (1, 3, 2):
        x_copies[d] = remote(tok_ref.at[:, cols(xto(d))], rows(zin, loc * tok_rows, tok_rows),
                             xs_sem.at[d - 1], xr_sem.at[d - 1], node, xto(d))
        x_copies[d].start()
    z_send(0, tok_ref.at[:, cols(loc)])
    w_copies = [
        pltpu.make_async_copy(wg_ref.at[0], wgu.at[:, pl.ds(0, ff)], w_sem.at[0]),
        pltpu.make_async_copy(wu_ref.at[0], wgu.at[:, pl.ds(ff, ff)], w_sem.at[1]),
        pltpu.make_async_copy(wd_ref.at[0], wd, w_sem.at[2]),
    ]
    meta[0, loc] = meta_ref[...]
    for d in (1, 3, 2):
        m_copies[d].wait()
    for r, dz in ((1, 1), (2, 3), (3, 2)):
        n_copies[r] = remote(meta.at[0], meta.at[r], ns_sem.at[r - 1], nr_sem.at[r - 1], at_node(dz, 0, 0), loc)
        n_copies[r].start()
    for w in w_copies:
        w.start()
    for d in (1, 3, 2):
        x_copies[d].wait_recv()
        z_send(d, rows(zin, ((loc + LOCALS - d) % LOCALS) * tok_rows, tok_rows))
    own_tok.wait()

    d_copies, p_copies, h_copies, a_copies = {}, {}, {}, {}

    def plane_send(r):
        if r > 0:
            n_copies[r].wait_recv()
        if r == 3:
            for d in (0, 1, 3, 2):
                o_copies[1, d].wait_recv()
                o_copies[2, d].wait_recv()
        at = lax.broadcasted_iota(jnp.int32, (slots, tok_rows), 0)
        for i in range(len(STEPS)):
            row_id = (at + at_node(0, *STEPS[i]) * slots).astype(F32)
            for b in range(LOCALS):
                d0 = meta[r, b, 0:1, :] + float(b * cap)
                d1 = meta[r, b, 1:2, :] + float(b * cap)
                hit = jnp.where(row_id == d0, 1.0, 0.0) + jnp.where(row_id == d1, 1.0, 0.0)
                pick[i * slots:(i + 1) * slots, b * tok_rows:(b + 1) * tok_rows] = hit.astype(BF16)

        @pl.loop(0, quarter // 256)
        def _(t):
            got = jnp.dot(pick[...], zin[r * ptok:(r + 1) * ptok, tile(t)], preferred_element_type=F32).astype(BF16)
            abuf[r * prows:r * prows + slots, tile(t)] = got[:slots]
            sbuf[r * prows + slots:(r + 1) * prows, tile(t)] = got[slots:]

        for i in range(1, len(STEPS)):
            at = pl.ds(r * prows + i * slots, slots)
            d_copies[r, i] = remote(sbuf.at[at], abuf.at[at], ds_sem.at[r, i], dr_sem.at[r, i],
                                    at_node(0, *STEPS[i]), loc)
            d_copies[r, i].start()

    def members(g):
        return [(g // HALVES, g % HALVES * PER + j) for j in range(PER)]

    def stage_a(g):
        for r, i in members(g):
            if i > 0:
                d_copies[r, i].wait_recv()
        if g == 0:
            w_copies[0].wait()
            w_copies[1].wait()

        @pl.loop(0, 2 * ff // 256)
        def _(t):
            part[...] = jnp.dot(abuf[g * grows:(g + 1) * grows, :], wgu[:, tile(t)], preferred_element_type=F32)
            pre[g * grows:(g + 1) * grows, tile(t)] = part[...].astype(BF16)
            ownf[g, :, tile(t)] = part[pl.ds(pl.multiple_of(loc * own, 16), own), :]

        for d in (2, 1, 3):
            p_copies[g, d] = remote(rows(pre, g * grows + xto(d) * own, own), rsbuf.at[g, d - 1],
                                    ps_sem.at[g, d - 1], pr_sem.at[g, d - 1], node, xto(d))
            p_copies[g, d].start()

    def stage_b(g):
        for d in (2, 1, 3):
            p_copies[g, d].wait_recv()
        mine = pl.ds(pl.multiple_of(g * grows + loc * own, 16), own)

        @pl.loop(0, ff // 256)
        def _(t):
            gate, up = ownf[g, :, tile(t)], ownf[g, :, tile(t, ff)]
            for d in range(3):
                gate = gate + rsbuf[g, d, :, tile(t)].astype(F32)
                up = up + rsbuf[g, d, :, tile(t, ff)].astype(F32)
            hid[mine, tile(t)] = (gate / (1.0 + jnp.exp(-gate)) * up).astype(BF16)

        for d in (2, 1, 3):
            h_copies[g, d] = remote(hid.at[mine], hid.at[mine], hs_sem.at[g, d - 1], hr_sem.at[g, d - 1],
                                    node, xto(d))
            h_copies[g, d].start()

    def stage_c(g):
        for d in (2, 1, 3):
            h_copies[g, d].wait_recv()
        if g == 0:
            w_copies[2].wait()

        @pl.loop(0, quarter // 256)
        def _(t):
            got = jnp.dot(hid[g * grows:(g + 1) * grows, :], wd[:, tile(t)],
                          preferred_element_type=F32).astype(BF16)
            if g == 0:
                rbuf[0:slots, tile(t)] = got[:slots]
                abuf[slots:grows, tile(t)] = got[slots:]
            else:
                abuf[g * grows:(g + 1) * grows, tile(t)] = got

        for r, i in members(g):
            if (r, i) != (0, 0):
                at = pl.ds(r * prows + i * slots, slots)
                a_copies[r, i] = remote(abuf.at[at], rbuf.at[at], as_sem.at[r, i], ar_sem.at[r, i], back(r, i), loc)
                a_copies[r, i].start()

    def stage_m(r):
        spot = lax.broadcasted_iota(jnp.int32, (tok_rows, prows), 1)
        slot_id = spot + expert(r, 0) * slots
        for i in range(1, len(STEPS)):
            slot_id = jnp.where(spot >= i * slots, spot + (expert(r, i) - i) * slots, slot_id)
        slot_id = slot_id.astype(F32)
        for b in range(LOCALS):
            m = jnp.transpose(meta[0, b])
            d0, d1 = m[:, 0:1] + float(b * cap), m[:, 1:2] + float(b * cap)
            w = jnp.where(slot_id == d0, m[:, 2:3], 0.0) + jnp.where(slot_id == d1, m[:, 3:4], 0.0)
            high = w.astype(BF16)
            uhi[b * tok_rows:(b + 1) * tok_rows, :] = high
            ulo[b * tok_rows:(b + 1) * tok_rows, :] = (w - high.astype(F32)).astype(BF16)
        for i in range(len(STEPS)):
            if (r, i) != (0, 0):
                a_copies[r, i].wait_recv()

        @pl.loop(0, quarter // 256)
        def _(t):
            got = rbuf[r * prows:(r + 1) * prows, tile(t)]
            mix = jnp.dot(uhi[...], got, preferred_element_type=F32) + jnp.dot(
                ulo[...], got, preferred_element_type=F32)
            if r > 0:
                mix = mix + acc[:, tile(t)]
            if r < len(PLANES) - 1:
                acc[:, tile(t)] = mix
            else:
                mbuf[:, tile(t)] = mix.astype(BF16)

    plane_send(0)
    z_forward(0)
    z_forward(1)
    z_forward(3)
    stage_a(0)
    stage_a(1)
    z_forward(2)
    plane_send(1)
    plane_send(2)
    stage_b(0)
    stage_b(1)
    stage_a(2)
    stage_c(0)
    stage_a(3)
    stage_c(1)
    plane_send(3)
    stage_b(2)
    stage_a(4)
    stage_b(3)
    stage_c(2)
    stage_a(5)
    stage_b(4)
    stage_c(3)
    stage_a(6)
    stage_b(5)
    stage_c(4)
    stage_a(7)
    stage_b(6)
    stage_c(5)
    stage_m(0)
    stage_b(7)
    stage_c(6)
    stage_c(7)
    stage_m(1)
    stage_m(2)
    stage_m(3)

    f_copies = []
    for d in (2, 1, 3):
        f_copies.append(remote(rows(mbuf, xto(d) * tok_rows, tok_rows), out_ref.at[:, cols(loc)],
                               fs_sem.at[d - 1], fr_sem.at[d - 1], node, xto(d)))
        f_copies[-1].start()
    own_out = pltpu.make_async_copy(rows(mbuf, loc * tok_rows, tok_rows), out_ref.at[:, cols(loc)], l_sem.at[1])
    own_out.start()
    for sent in (x_copies, n_copies, z_copies, o_copies, d_copies, a_copies, p_copies, h_copies):
        for copy in sent.values():
            copy.wait_send()
    own_out.wait()
    for f in f_copies:
        f.wait()


def shards(tokens, node_set, gate_weights, w_gate, w_up, w_down):
    tok_rows, width = tokens.shape
    quarter = width // LOCALS
    ff = w_gate.shape[2]
    routes = node_set.shape[1]
    cap = 3 * tok_rows * routes // (2 * NODES)
    slots = LOCALS * cap
    total = NODES * slots
    prows = len(STEPS) * slots
    grows = PER * slots
    own = grows // LOCALS

    member = node_set[:, :, None] == jnp.arange(NODES, dtype=jnp.int32)[None, None, :]
    counts = jnp.sum(member.astype(F32), axis=1)
    earlier = jnp.tri(tok_rows, k=-1, dtype=BF16)
    before = jnp.dot(earlier, counts.astype(BF16), preferred_element_type=F32)
    slot = jnp.sum(jnp.where(member, before[:, None, :], 0.0), axis=2)
    dest = (node_set * slots).astype(F32) + slot
    meta = jnp.concatenate([dest.T, gate_weights.T, jnp.zeros((4, tok_rows), F32)], axis=0)

    any_spec = pl.BlockSpec(memory_space=pl.ANY)
    dma = pltpu.SemaphoreType.DMA
    return pl.pallas_call(
        functools.partial(kernel, tok_rows, quarter, ff, cap),
        name="routed_experts",
        out_shape=jax.ShapeDtypeStruct((tok_rows, width), BF16),
        in_specs=[pl.BlockSpec(memory_space=pltpu.VMEM)] + [any_spec] * 4,
        out_specs=any_spec,
        scratch_shapes=[
            pltpu.VMEM((len(PLANES), LOCALS, 8, tok_rows), F32),
            pltpu.VMEM((len(PLANES) * LOCALS * tok_rows, quarter), BF16),
            pltpu.VMEM((prows, LOCALS * tok_rows), BF16),
            pltpu.VMEM((total, quarter), BF16),
            pltpu.VMEM((total, quarter), BF16),
            pltpu.VMEM((quarter, 2 * ff), BF16),
            pltpu.VMEM((ff, quarter), BF16),
            pltpu.VMEM((total, 2 * ff), BF16),
            pltpu.VMEM((grows, 256), F32),
            pltpu.VMEM((GROUPS, own, 2 * ff), F32),
            pltpu.VMEM((GROUPS, LOCALS - 1, own, 2 * ff), BF16),
            pltpu.VMEM((total, ff), BF16),
            pltpu.VMEM((total, quarter), BF16),
            pltpu.VMEM((LOCALS * tok_rows, prows), BF16),
            pltpu.VMEM((LOCALS * tok_rows, prows), BF16),
            pltpu.VMEM((LOCALS * tok_rows, quarter), F32),
            pltpu.VMEM((LOCALS * tok_rows, quarter), BF16),
            dma((3,)), dma((2,)), dma((3,)), dma((3,)), dma((3,)), dma((3,)), dma((3,)), dma((3,)),
            dma((2, 4)), dma((2, 4)), dma((2, 4)), dma((2, 4)),
            dma((4, 8)), dma((4, 8)),
            dma((GROUPS, 3)), dma((GROUPS, 3)), dma((GROUPS, 3)), dma((GROUPS, 3)),
            dma((4, 8)), dma((4, 8)), dma((3,)), dma((3,)),
        ],
        compiler_params=pltpu.CompilerParams(
            collective_id=0, has_side_effects=True, vmem_limit_bytes=62 * 2**20),
        cost_estimate=pl.CostEstimate(flops=20 * 10**9, bytes_accessed=15 * 10**6, transcendentals=10**6),
    )(meta, tokens, w_gate, w_up, w_down)


def solution(mesh):
    placed = (
        P(("node", "local"), None),
        P(("node", "local"), None),
        P(("node", "local"), None),
        P("node", "local", None),
        P("node", "local", None),
        P("node", None, "local"),
    )
    return jax.shard_map(
        shards, mesh=mesh, in_specs=placed, out_specs=P(("node", "local"), None), check_vma=False
    )
```

time: 260 us -> 225 us (0.87)
  the two profiles are of different devices: /device:TPU:48 before, /device:TPU:1 now
where the time goes in v2:
time: 225 us
  Pallas kernels  218 us (97%)
  other arithmetic  3.43 us (2%)
  local copies, waits for them, and re-layouts  2.92 us (1%)
    pallas_call x1, Pallas kernels, shards(): pl.pallas_call(functools.partial(kernel, tok_rows, quarter, ff, cap), nam...  218 us

profile of v2, /device:TPU:1, one launch (start us, length us, event | category | flops | bytes accessed | tf_op | source)
XLA Modules:
  0.0 224.6 jit_solution(11025005893537041673)
XLA Ops:
  0.0 0.1 pad.2.clone
  0.1 0.7 convert_reduce_fusion
  0.8 0.2 fusion
  1.0 0.7 select_reduce_fusion
  1.7 0.7 add_bitcast_fusion
  2.4 1.3 maximum_maximum_fusion.meta_ref
  3.7 218.0 %routed_experts.1 = bf16[128,7168]{1,0:T(8,128)(2,1)} custom-call(f32[8,128]{1,0:T(8,128)} %maximum_maximum_fusion.meta_ref, bf16[128,7168]{1,0:T(8,128)(2,1)} %tok_ref.1, bf16[1,1792,1024]{2,1,0:T(8,128)(2,1)} %wg_ref.1, bf16[1,1792,1024]{2,1,0:T(8,128)(2,1)} %wu_ref.1, bf16[1,1024,1792]{2,1,0:T(8,128)(2,1)} %wd_ref.1), custom_call_target="tpu_custom_call" | custom-call | flops 20000000000 | bytes 15000000 | tf_op jit(solution)/shard_map/routed_experts/pallas_call | solution.py:311
  221.7 2.8 %copy.10 = bf16[128,7168]{1,0:T(8,128)(2,1)} copy(bf16[128,7168]{1,0:T(8,128)(2,1)} %routed_experts.1) | data formatting | bytes 3670016
  (2 shorter events, 0.0 us)

commit v3 on v2

--- a/solution.py
+++ b/solution.py
@@ -16,17 +16,19 @@
 HALVES = 2
 PER = len(STEPS) // HALVES
 GROUPS = len(PLANES) * HALVES
+PARTS = ((0, 3), (3, 7))
 
 
 def kernel(tok_rows, quarter, ff, cap,
-           meta_ref, tok_ref, wg_ref, wu_ref, wd_ref, out_ref,
-           meta, zin, pick, sbuf, abuf, wgu, wd, pre, part, ownf, rsbuf, hid, rbuf, uhi, ulo, acc, mbuf,
-           w_sem, l_sem, ms_sem, mr_sem, ns_sem, nr_sem, xs_sem, xr_sem, zs_sem, zr_sem, os_sem, or_sem,
+           set_ref, gw_ref, tok_ref, wg_ref, wu_ref, wd_ref, out_ref,
+           meta, zin, pick, sbuf, abuf, wgu, wd, pre, part, ownf, nearf, fbuf, rsbuf, hid, rbuf, uhi, ulo, acc, mbuf,
+           w_sem, l_sem, o_sem, ms_sem, mr_sem, ns_sem, nr_sem, xs_sem, xr_sem, zs_sem, zr_sem, os_sem, or_sem,
            ds_sem, dr_sem, ps_sem, pr_sem, hs_sem, hr_sem, as_sem, ar_sem, fs_sem, fr_sem):
     slots = LOCALS * cap
     prows = len(STEPS) * slots
     grows = PER * slots
     own = grows // LOCALS
+    fh = ff // 2
     ptok = LOCALS * tok_rows
     node, loc = lax.axis_index("node"), lax.axis_index("local")
     z, y, c = node // 8, (node // 2) % 4, node % 2
@@ -67,11 +69,20 @@
         pl.semaphore_signal(barrier, inc=1, device_id=(node, xto(d)), device_id_type=MESH)
     own_tok = pltpu.make_async_copy(tok_ref.at[:, cols(loc)], rows(zin, loc * tok_rows, tok_rows), l_sem.at[0])
     own_tok.start()
+    names = lax.broadcasted_iota(jnp.int32, (NODES, tok_rows), 0)
+    member = [jnp.where(names == set_ref[r:r + 1, :], 1.0, 0.0) for r in range(2)]
+    row, col = (lax.broadcasted_iota(jnp.int32, (tok_rows, tok_rows), k) for k in range(2))
+    before = jnp.dot((member[0] + member[1]).astype(BF16), jnp.where(row < col, 1.0, 0.0).astype(BF16),
+                     preferred_element_type=F32)
+    for r in range(2):
+        slot = jnp.sum(member[r] * before, axis=0, keepdims=True)
+        meta[0, loc, r:r + 1, :] = (set_ref[r:r + 1, :] * slots).astype(F32) + slot
+    meta[0, loc, 2:4, :] = gw_ref[...]
     pl.semaphore_wait(barrier, NODES - 1 + LOCALS - 1)
 
     m_copies, n_copies, x_copies, z_copies, o_copies = {}, {}, {}, {}, {}
     for d in (1, 3, 2):
-        m_copies[d] = remote(meta_ref, meta.at[0, loc], ms_sem.at[d - 1], mr_sem.at[d - 1], node, xto(d))
+        m_copies[d] = remote(meta.at[0, loc], meta.at[0, loc], ms_sem.at[d - 1], mr_sem.at[d - 1], node, xto(d))
         m_copies[d].start()
 
     def z_send(d, src):
@@ -81,11 +92,18 @@
                                     at_node(dz, 0, 0), loc)
             z_copies[r, d].start()
 
+    arrived = set()
+
+    def z_arrive(r, d):
+        if (r, d) not in arrived:
+            arrived.add((r, d))
+            z_copies[r, d].wait_recv()
+
     def z_forward(d):
         half = tok_rows // 2
         at = ((loc + LOCALS - d) % LOCALS) * tok_rows
         for r, dz, shift in ((1, 1, 0), (2, 3, half)):
-            z_copies[r, d].wait_recv()
+            z_arrive(r, d)
             o_copies[r, d] = remote(rows(zin, r * ptok + at + shift, half), rows(zin, 3 * ptok + at + shift, half),
                                     os_sem.at[r - 1, d], or_sem.at[r - 1, d], at_node(dz, 0, 0), loc)
             o_copies[r, d].start()
@@ -96,11 +114,11 @@
         x_copies[d].start()
     z_send(0, tok_ref.at[:, cols(loc)])
     w_copies = [
-        pltpu.make_async_copy(wg_ref.at[0], wgu.at[:, pl.ds(0, ff)], w_sem.at[0]),
-        pltpu.make_async_copy(wu_ref.at[0], wgu.at[:, pl.ds(ff, ff)], w_sem.at[1]),
-        pltpu.make_async_copy(wd_ref.at[0], wd, w_sem.at[2]),
+        pltpu.make_async_copy(ref.at[0, :, pl.ds(k * fh, fh)], wgu.at[:, pl.ds(k * ff + u * fh, fh)], w_sem.at[k, u])
+        for k in range(2) for u, ref in enumerate((wg_ref, wu_ref))
+    ] + [
+        pltpu.make_async_copy(wd_ref.at[0], wd, w_sem.at[2, 0]),
     ]
-    meta[0, loc] = meta_ref[...]
     for d in (1, 3, 2):
         m_copies[d].wait()
     for r, dz in ((1, 1), (2, 3), (3, 2)):
@@ -114,10 +132,14 @@
     own_tok.wait()
 
     d_copies, p_copies, h_copies, a_copies = {}, {}, {}, {}
+    seen = []
 
     def plane_send(r):
         if r > 0:
             n_copies[r].wait_recv()
+        if r in (1, 2):
+            for d in range(LOCALS):
+                z_arrive(r, d)
         if r == 3:
             for d in (0, 1, 3, 2):
                 o_copies[1, d].wait_recv()
@@ -146,48 +168,84 @@
     def members(g):
         return [(g // HALVES, g % HALVES * PER + j) for j in range(PER)]
 
+    def mine(g, d):
+        return pl.ds(pl.multiple_of(g * grows + xto(d) * own, 16), own)
+
+    def p_send(g, k, src, dst, d):
+        p_copies[g, k] = remote(src, dst, ps_sem.at[g, k], pr_sem.at[g, k], node, xto(d))
+        p_copies[g, k].start()
+
+    first, second = pl.ds(0, ff), pl.ds(ff, ff)
+
     def stage_a(g):
         for r, i in members(g):
             if i > 0:
                 d_copies[r, i].wait_recv()
-        if g == 0:
-            w_copies[0].wait()
-            w_copies[1].wait()
+        if "a" not in seen:
+            seen.append("a")
+            for w in w_copies[:4]:
+                w.wait()
 
         @pl.loop(0, 2 * ff // 256)
         def _(t):
             part[...] = jnp.dot(abuf[g * grows:(g + 1) * grows, :], wgu[:, tile(t)], preferred_element_type=F32)
             pre[g * grows:(g + 1) * grows, tile(t)] = part[...].astype(BF16)
             ownf[g, :, tile(t)] = part[pl.ds(pl.multiple_of(loc * own, 16), own), :]
-
-        for d in (2, 1, 3):
-            p_copies[g, d] = remote(rows(pre, g * grows + xto(d) * own, own), rsbuf.at[g, d - 1],
-                                    ps_sem.at[g, d - 1], pr_sem.at[g, d - 1], node, xto(d))
-            p_copies[g, d].start()
+            near = (loc + 1 + 2 * (t // (ff // 256))) % LOCALS
+            nearf[g, :, tile(t)] = part[pl.ds(pl.multiple_of(near * own, 16), own), :]
+
+        p_send(g, 0, pre.at[mine(g, 2), first], fbuf.at[g, 0], 1)
+        p_send(g, 1, pre.at[mine(g, 2), second], fbuf.at[g, 1], 3)
+        p_send(g, 2, pre.at[mine(g, 1), second], rsbuf.at[g, 0, :, second], 1)
+        p_send(g, 3, pre.at[mine(g, 3), first], rsbuf.at[g, 1, :, first], 3)
+
+    def stage_s(g):
+        for k, d, at in ((0, 1, first), (1, 3, second)):
+            p_copies[g, k].wait_recv()
+            pre[mine(g, d), at] = (nearf[g, :, at] + fbuf[g, k].astype(F32)).astype(BF16)
+            p_send(g, 4 + k, pre.at[mine(g, d), at], rsbuf.at[g, k, :, at], d)
+
+    def h_send(g, k, ref, d):
+        h_copies[g, k] = remote(ref, ref, hs_sem.at[g, k], hr_sem.at[g, k], node, xto(d))
+        h_copies[g, k].start()
 
     def stage_b(g):
-        for d in (2, 1, 3):
-            p_copies[g, d].wait_recv()
-        mine = pl.ds(pl.multiple_of(g * grows + loc * own, 16), own)
+        for k in (2, 3, 4, 5):
+            p_copies[g, k].wait_recv()
 
         @pl.loop(0, ff // 256)
         def _(t):
-            gate, up = ownf[g, :, tile(t)], ownf[g, :, tile(t, ff)]
-            for d in range(3):
-                gate = gate + rsbuf[g, d, :, tile(t)].astype(F32)
-                up = up + rsbuf[g, d, :, tile(t, ff)].astype(F32)
-            hid[mine, tile(t)] = (gate / (1.0 + jnp.exp(-gate)) * up).astype(BF16)
-
-        for d in (2, 1, 3):
-            h_copies[g, d] = remote(hid.at[mine], hid.at[mine], hs_sem.at[g, d - 1], hr_sem.at[g, d - 1],
-                                    node, xto(d))
-            h_copies[g, d].start()
+            at_gate = pl.ds(pl.multiple_of(t // 2 * ff + t % 2 * 256, 256), 256)
+            at_up = pl.ds(pl.multiple_of(t // 2 * ff + t % 2 * 256 + fh, 256), 256)
+            gate, up = ownf[g, :, at_gate], ownf[g, :, at_up]
+            for k in range(2):
+                gate = gate + rsbuf[g, k, :, at_gate].astype(F32)
+                up = up + rsbuf[g, k, :, at_up].astype(F32)
+            hid[mine(g, 0), tile(t)] = (gate / (1.0 + jnp.exp(-gate)) * up).astype(BF16)
+
+        h_send(g, 0, hid.at[mine(g, 0)], 1)
+        h_send(g, 1, hid.at[mine(g, 0)], 3)
+
+    def stage_w(g):
+        h_copies[g, 0].wait_recv()
+        h_send(g, 2, hid.at[mine(g, 3), pl.ds(0, fh)], 1)
+        h_copies[g, 1].wait_recv()
+        h_send(g, 3, hid.at[mine(g, 1), pl.ds(fh, fh)], 3)
+
+    def a_send(g, k, lo, hi):
+        for r, i in members(g):
+            if (r, i) != (0, 0):
+                at = pl.ds(r * prows + i * slots, slots), pl.ds(lo * 256, (hi - lo) * 256)
+                a_copies[r, i, k] = remote(abuf.at[at], rbuf.at[at], as_sem.at[k, r, i], ar_sem.at[k, r, i],
+                                           back(r, i), loc)
+                a_copies[r, i, k].start()
 
     def stage_c(g):
-        for d in (2, 1, 3):
-            h_copies[g, d].wait_recv()
-        if g == 0:
-            w_copies[2].wait()
+        h_copies[g, 2].wait_recv()
+        h_copies[g, 3].wait_recv()
+        if "c" not in seen:
+            seen.append("c")
+            w_copies[4].wait()
 
         @pl.loop(0, quarter // 256)
         def _(t):
@@ -199,11 +257,14 @@
             else:
                 abuf[g * grows:(g + 1) * grows, tile(t)] = got
 
-        for r, i in members(g):
-            if (r, i) != (0, 0):
-                at = pl.ds(r * prows + i * slots, slots)
-                a_copies[r, i] = remote(abuf.at[at], rbuf.at[at], as_sem.at[r, i], ar_sem.at[r, i], back(r, i), loc)
-                a_copies[r, i].start()
+        if g < GROUPS - HALVES:
+            a_send(g, 0, 0, quarter // 256)
+        else:
+            a_send(g, 0, *PARTS[0])
+        if g == GROUPS - 1:
+            for k in range(1, len(PARTS)):
+                for h in range(GROUPS - HALVES, GROUPS):
+                    a_send(h, k, *PARTS[k])
 
     def stage_m(r):
         spot = lax.broadcasted_iota(jnp.int32, (tok_rows, prows), 1)
@@ -218,72 +279,94 @@
             high = w.astype(BF16)
             uhi[b * tok_rows:(b + 1) * tok_rows, :] = high
             ulo[b * tok_rows:(b + 1) * tok_rows, :] = (w - high.astype(F32)).astype(BF16)
-        for i in range(len(STEPS)):
-            if (r, i) != (0, 0):
-                a_copies[r, i].wait_recv()
-
-        @pl.loop(0, quarter // 256)
-        def _(t):
-            got = rbuf[r * prows:(r + 1) * prows, tile(t)]
-            mix = jnp.dot(uhi[...], got, preferred_element_type=F32) + jnp.dot(
-                ulo[...], got, preferred_element_type=F32)
-            if r > 0:
-                mix = mix + acc[:, tile(t)]
+        for k, (lo, hi) in enumerate(PARTS if r == len(PLANES) - 1 else ((0, quarter // 256),)):
+            for i in range(len(STEPS)):
+                if (r, i) != (0, 0):
+                    a_copies[r, i, k].wait_recv()
+
+            @pl.loop(lo, hi)
+            def _(t):
+                got = rbuf[r * prows:(r + 1) * prows, tile(t)]
+                mix = jnp.dot(uhi[...], got, preferred_element_type=F32) + jnp.dot(
+                    ulo[...], got, preferred_element_type=F32)
+                if "m" in seen:
+                    mix = mix + acc[:, tile(t)]
+                if r < len(PLANES) - 1:
+                    acc[:, tile(t)] = mix
+                else:
+                    mbuf[:, tile(t)] = mix.astype(BF16)
+
             if r < len(PLANES) - 1:
-                acc[:, tile(t)] = mix
+                seen.append("m")
             else:
-                mbuf[:, tile(t)] = mix.astype(BF16)
-
-    plane_send(0)
+                here = pl.ds(pl.multiple_of(loc * quarter + lo * 256, 256), (hi - lo) * 256)
+                for d in (2, 1, 3):
+                    at = pl.ds(pl.multiple_of(xto(d) * tok_rows, 16), tok_rows), pl.ds(lo * 256, (hi - lo) * 256)
+                    f_copies[k, d] = remote(mbuf.at[at], out_ref.at[:, here], fs_sem.at[k, d - 1], fr_sem.at[k, d - 1],
+                                            node, xto(d))
+                    f_copies[k, d].start()
+                at = pl.ds(pl.multiple_of(loc * tok_rows, 16), tok_rows), pl.ds(lo * 256, (hi - lo) * 256)
+                own_out.append(pltpu.make_async_copy(mbuf.at[at], out_ref.at[:, here], o_sem.at[k]))
+                own_out[-1].start()
+
+    f_copies, own_out = {}, []
     z_forward(0)
     z_forward(1)
+    plane_send(0)
+    stage_a(0)
+    plane_send(1)
+    stage_a(1)
+    plane_send(2)
+    z_forward(2)
+    stage_s(1)
     z_forward(3)
-    stage_a(0)
-    stage_a(1)
-    z_forward(2)
-    plane_send(1)
-    plane_send(2)
-    stage_b(0)
+    stage_a(2)
     stage_b(1)
-    stage_a(2)
-    stage_c(0)
+    stage_s(2)
     stage_a(3)
-    stage_c(1)
-    plane_send(3)
     stage_b(2)
     stage_a(4)
+    plane_send(3)
+    stage_w(2)
+    stage_s(4)
+    stage_a(5)
+    stage_c(2)
+    stage_b(4)
+    stage_s(3)
+    stage_w(4)
+    stage_s(5)
     stage_b(3)
-    stage_c(2)
-    stage_a(5)
-    stage_b(4)
+    stage_s(0)
+    stage_c(4)
+    stage_b(5)
+    stage_w(3)
+    stage_a(6)
+    stage_w(5)
+    stage_w(1)
     stage_c(3)
-    stage_a(6)
-    stage_b(5)
-    stage_c(4)
+    stage_s(6)
+    stage_b(0)
+    stage_c(5)
+    stage_b(6)
     stage_a(7)
-    stage_b(6)
-    stage_c(5)
+    stage_w(6)
+    stage_w(0)
+    stage_s(7)
+    stage_c(1)
+    stage_c(6)
+    stage_b(7)
+    stage_m(1)
+    stage_w(7)
+    stage_c(0)
+    stage_c(7)
+    stage_m(2)
     stage_m(0)
-    stage_b(7)
-    stage_c(6)
-    stage_c(7)
-    stage_m(1)
-    stage_m(2)
     stage_m(3)
-
-    f_copies = []
-    for d in (2, 1, 3):
-        f_copies.append(remote(rows(mbuf, xto(d) * tok_rows, tok_rows), out_ref.at[:, cols(loc)],
-                               fs_sem.at[d - 1], fr_sem.at[d - 1], node, xto(d)))
-        f_copies[-1].start()
-    own_out = pltpu.make_async_copy(rows(mbuf, loc * tok_rows, tok_rows), out_ref.at[:, cols(loc)], l_sem.at[1])
-    own_out.start()
     for sent in (x_copies, n_copies, z_copies, o_copies, d_copies, a_copies, p_copies, h_copies):
         for copy in sent.values():
             copy.wait_send()
-    own_out.wait()
-    for f in f_copies:
-        f.wait()
+    for copy in own_out + list(f_copies.values()):
+        copy.wait()
 
 
 def shards(tokens, node_set, gate_weights, w_gate, w_up, w_down):
@@ -298,21 +381,13 @@
     grows = PER * slots
     own = grows // LOCALS
 
-    member = node_set[:, :, None] == jnp.arange(NODES, dtype=jnp.int32)[None, None, :]
-    counts = jnp.sum(member.astype(F32), axis=1)
-    earlier = jnp.tri(tok_rows, k=-1, dtype=BF16)
-    before = jnp.dot(earlier, counts.astype(BF16), preferred_element_type=F32)
-    slot = jnp.sum(jnp.where(member, before[:, None, :], 0.0), axis=2)
-    dest = (node_set * slots).astype(F32) + slot
-    meta = jnp.concatenate([dest.T, gate_weights.T, jnp.zeros((4, tok_rows), F32)], axis=0)
-
     any_spec = pl.BlockSpec(memory_space=pl.ANY)
     dma = pltpu.SemaphoreType.DMA
     return pl.pallas_call(
         functools.partial(kernel, tok_rows, quarter, ff, cap),
         name="routed_experts",
         out_shape=jax.ShapeDtypeStruct((tok_rows, width), BF16),
-        in_specs=[pl.BlockSpec(memory_space=pltpu.VMEM)] + [any_spec] * 4,
+        in_specs=[pl.BlockSpec(memory_space=pltpu.VMEM)] * 2 + [any_spec] * 4,
         out_specs=any_spec,
         scratch_shapes=[
             pltpu.VMEM((len(PLANES), LOCALS, 8, tok_rows), F32),
@@ -325,23 +400,26 @@
             pltpu.VMEM((total, 2 * ff), BF16),
             pltpu.VMEM((grows, 256), F32),
             pltpu.VMEM((GROUPS, own, 2 * ff), F32),
-            pltpu.VMEM((GROUPS, LOCALS - 1, own, 2 * ff), BF16),
+            pltpu.VMEM((GROUPS, own, 2 * ff), F32),
+            pltpu.VMEM((GROUPS, 2, own, ff), BF16),
+            pltpu.VMEM((GROUPS, 2, own, 2 * ff), BF16),
             pltpu.VMEM((total, ff), BF16),
             pltpu.VMEM((total, quarter), BF16),
             pltpu.VMEM((LOCALS * tok_rows, prows), BF16),
             pltpu.VMEM((LOCALS * tok_rows, prows), BF16),
             pltpu.VMEM((LOCALS * tok_rows, quarter), F32),
             pltpu.VMEM((LOCALS * tok_rows, quarter), BF16),
-            dma((3,)), dma((2,)), dma((3,)), dma((3,)), dma((3,)), dma((3,)), dma((3,)), dma((3,)),
+            dma((3, 2)), dma((1,)), dma((len(PARTS),)),
+            dma((3,)), dma((3,)), dma((3,)), dma((3,)), dma((3,)), dma((3,)),
             dma((2, 4)), dma((2, 4)), dma((2, 4)), dma((2, 4)),
             dma((4, 8)), dma((4, 8)),
-            dma((GROUPS, 3)), dma((GROUPS, 3)), dma((GROUPS, 3)), dma((GROUPS, 3)),
-            dma((4, 8)), dma((4, 8)), dma((3,)), dma((3,)),
+            dma((GROUPS, 6)), dma((GROUPS, 6)), dma((GROUPS, 4)), dma((GROUPS, 4)),
+            dma((len(PARTS), 4, 8)), dma((len(PARTS), 4, 8)), dma((len(PARTS), 3)), dma((len(PARTS), 3)),
         ],
         compiler_params=pltpu.CompilerParams(
             collective_id=0, has_side_effects=True, vmem_limit_bytes=62 * 2**20),
         cost_estimate=pl.CostEstimate(flops=20 * 10**9, bytes_accessed=15 * 10**6, transcendentals=10**6),
-    )(meta, tokens, w_gate, w_up, w_down)
+    )(node_set.T, gate_weights.T, tokens, w_gate, w_up, w_down)
 
 
 def solution(mesh):

time: 225 us -> 201 us (0.89); the launches traced: 225 us -> 198 us
  Pallas kernels: 218 us -> 195 us
  other arithmetic: 3.43 us -> 0 us
    pallas_call x1, Pallas kernels: 218 us -> 195 us  [shards(): pl.pallas_call(functools.partial(kernel, tok_rows, quarter, ff, cap), nam...]
where the time goes in v3:
time: 201 us; the launch traced here: 198 us
  Pallas kernels  195 us (97%)
  local copies, waits for them, and re-layouts  2.85 us (1%)
    pallas_call x1, Pallas kernels, shards(): pl.pallas_call(functools.partial(kernel, tok_rows, quarter, ff, cap), nam...  195 us

profile of v3, /device:TPU:1, one launch (start us, length us, event | category | flops | bytes accessed | tf_op | source)
XLA Modules:
  0.0 198.2 jit_solution(3841302482215618500)
XLA Ops:
  0.0 195.4 %routed_experts.1 = bf16[128,7168]{1,0:T(8,128)(2,1)} custom-call(s32[2,128]{1,0:T(2,128)} %bitcast.2, f32[2,128]{1,0:T(2,128)} %bitcast.3, bf16[128,7168]{1,0:T(8,128)(2,1)} %tok_ref.1, bf16[1,1792,1024]{2,1,0:T(8,128)(2,1)} %wg_ref.1, bf16[1,1792,1024]{2,1,0:T(8,128)(2,1)} %wu_ref.1, bf16[1,1024,1792]{2,1,0:T(8,128)(2,1)} %wd_ref.1), custom_call_target="tpu_custom_call" | custom-call | flops 20000000000 | bytes 15000000 | tf_op jit(solution)/shard_map/routed_experts/pallas_call | solution.py:386
  195.4 2.8 %copy.8 = bf16[128,7168]{1,0:T(8,128)(2,1)} copy(bf16[128,7168]{1,0:T(8,128)(2,1)} %routed_experts.1) | data formatting | bytes 3670016

commit v4 on v3

--- a/solution.py
+++ b/solution.py
@@ -16,7 +16,7 @@
 HALVES = 2
 PER = len(STEPS) // HALVES
 GROUPS = len(PLANES) * HALVES
-PARTS = ((0, 3), (3, 7))
+PARTS = ((0, 2), (2, 4), (4, 7))
 
 
 def kernel(tok_rows, quarter, ff, cap,
@@ -159,7 +159,13 @@
             abuf[r * prows:r * prows + slots, tile(t)] = got[:slots]
             sbuf[r * prows + slots:(r + 1) * prows, tile(t)] = got[slots:]
 
-        for i in range(1, len(STEPS)):
+        plane_copies(r, range(1, PER))
+
+    def plane_more(r):
+        plane_copies(r, range(PER, len(STEPS)))
+
+    def plane_copies(r, which):
+        for i in which:
             at = pl.ds(r * prows + i * slots, slots)
             d_copies[r, i] = remote(sbuf.at[at], abuf.at[at], ds_sem.at[r, i], dr_sem.at[r, i],
                                     at_node(0, *STEPS[i]), loc)
@@ -196,21 +202,19 @@
 
         p_send(g, 0, pre.at[mine(g, 2), first], fbuf.at[g, 0], 1)
         p_send(g, 1, pre.at[mine(g, 2), second], fbuf.at[g, 1], 3)
-        p_send(g, 2, pre.at[mine(g, 1), second], rsbuf.at[g, 0, :, second], 1)
-        p_send(g, 3, pre.at[mine(g, 3), first], rsbuf.at[g, 1, :, first], 3)
 
     def stage_s(g):
         for k, d, at in ((0, 1, first), (1, 3, second)):
             p_copies[g, k].wait_recv()
             pre[mine(g, d), at] = (nearf[g, :, at] + fbuf[g, k].astype(F32)).astype(BF16)
-            p_send(g, 4 + k, pre.at[mine(g, d), at], rsbuf.at[g, k, :, at], d)
+            p_send(g, 2 + k, pre.at[mine(g, d)], rsbuf.at[g, k], d)
 
     def h_send(g, k, ref, d):
         h_copies[g, k] = remote(ref, ref, hs_sem.at[g, k], hr_sem.at[g, k], node, xto(d))
         h_copies[g, k].start()
 
     def stage_b(g):
-        for k in (2, 3, 4, 5):
+        for k in (2, 3):
             p_copies[g, k].wait_recv()
 
         @pl.loop(0, ff // 256)
@@ -261,10 +265,16 @@
             a_send(g, 0, 0, quarter // 256)
         else:
             a_send(g, 0, *PARTS[0])
-        if g == GROUPS - 1:
-            for k in range(1, len(PARTS)):
-                for h in range(GROUPS - HALVES, GROUPS):
-                    a_send(h, k, *PARTS[k])
+
+    left = set()
+
+    def last_parts(k):
+        if k >= 9:
+            for r, i in members(GROUPS - 2) + members(GROUPS - 1):
+                a_copies[r, i, k - 2].wait_send()
+                left.add((r, i, k - 2))
+        for h in range(GROUPS - HALVES, GROUPS):
+            a_send(h, k, *PARTS[k])
 
     def stage_m(r):
         spot = lax.broadcasted_iota(jnp.int32, (tok_rows, prows), 1)
@@ -313,10 +323,13 @@
     z_forward(0)
     z_forward(1)
     plane_send(0)
+    plane_more(0)
     stage_a(0)
     plane_send(1)
+    plane_more(1)
     stage_a(1)
     plane_send(2)
+    plane_more(2)
     z_forward(2)
     stage_s(1)
     z_forward(3)
@@ -327,6 +340,7 @@
     stage_b(2)
     stage_a(4)
     plane_send(3)
+    plane_more(3)
     stage_w(2)
     stage_s(4)
     stage_a(5)
@@ -359,11 +373,16 @@
     stage_w(7)
     stage_c(0)
     stage_c(7)
+    last_parts(1)
+    last_parts(2)
     stage_m(2)
     stage_m(0)
     stage_m(3)
-    for sent in (x_copies, n_copies, z_copies, o_copies, d_copies, a_copies, p_copies, h_copies):
+    for sent in (x_copies, n_copies, z_copies, o_copies, d_copies, p_copies, h_copies):
         for copy in sent.values():
+            copy.wait_send()
+    for key, copy in a_copies.items():
+        if key not in left:
             copy.wait_send()
     for copy in own_out + list(f_copies.values()):
         copy.wait()
@@ -413,7 +432,7 @@
             dma((3,)), dma((3,)), dma((3,)), dma((3,)), dma((3,)), dma((3,)),
             dma((2, 4)), dma((2, 4)), dma((2, 4)), dma((2, 4)),
             dma((4, 8)), dma((4, 8)),
-            dma((GROUPS, 6)), dma((GROUPS, 6)), dma((GROUPS, 4)), dma((GROUPS, 4)),
+            dma((GROUPS, 4)), dma((GROUPS, 4)), dma((GROUPS, 4)), dma((GROUPS, 4)),
             dma((len(PARTS), 4, 8)), dma((len(PARTS), 4, 8)), dma((len(PARTS), 3)), dma((len(PARTS), 3)),
         ],
         compiler_params=pltpu.CompilerParams(

time: 201 us -> 199 us (0.990); the launches traced: 198 us -> 199 us
  no operation moved by 1% of the time
where the time goes in v4:
time: 199 us
  Pallas kernels  196 us (98%)
  local copies, waits for them, and re-layouts  2.85 us (1%)
    pallas_call x1, Pallas kernels, shards(): pl.pallas_call(functools.partial(kernel, tok_rows, quarter, ff, cap), nam...  196 us

profile of v4, /device:TPU:1, one launch (start us, length us, event | category | flops | bytes accessed | tf_op | source)
XLA Modules:
  0.0 199.0 jit_solution(15447735735144872913)
XLA Ops:
  0.0 196.1 %routed_experts.1 = bf16[128,7168]{1,0:T(8,128)(2,1)} custom-call(s32[2,128]{1,0:T(2,128)} %bitcast.2, f32[2,128]{1,0:T(2,128)} %bitcast.3, bf16[128,7168]{1,0:T(8,128)(2,1)} %tok_ref.1, bf16[1,1792,1024]{2,1,0:T(8,128)(2,1)} %wg_ref.1, bf16[1,1792,1024]{2,1,0:T(8,128)(2,1)} %wu_ref.1, bf16[1,1024,1792]{2,1,0:T(8,128)(2,1)} %wd_ref.1), custom_call_target="tpu_custom_call" | custom-call | flops 20000000000 | bytes 15000000 | tf_op jit(solution)/shard_map/routed_experts/pallas_call | solution.py:405
  196.1 2.8 %copy.8 = bf16[128,7168]{1,0:T(8,128)(2,1)} copy(bf16[128,7168]{1,0:T(8,128)(2,1)} %routed_experts.1) | data formatting | bytes 3670016

commit v5 on v4

--- a/solution.py
+++ b/solution.py
@@ -328,12 +328,14 @@
     plane_send(1)
     plane_more(1)
     stage_a(1)
+    stage_s(0)
     plane_send(2)
     plane_more(2)
     z_forward(2)
     stage_s(1)
     z_forward(3)
     stage_a(2)
+    stage_b(0)
     stage_b(1)
     stage_s(2)
     stage_a(3)
@@ -341,6 +343,7 @@
     stage_a(4)
     plane_send(3)
     plane_more(3)
+    stage_w(0)
     stage_w(2)
     stage_s(4)
     stage_a(5)
@@ -350,7 +353,6 @@
     stage_w(4)
     stage_s(5)
     stage_b(3)
-    stage_s(0)
     stage_c(4)
     stage_b(5)
     stage_w(3)
@@ -359,22 +361,20 @@
     stage_w(1)
     stage_c(3)
     stage_s(6)
-    stage_b(0)
     stage_c(5)
     stage_b(6)
     stage_a(7)
     stage_w(6)
-    stage_w(0)
     stage_s(7)
     stage_c(1)
     stage_c(6)
     stage_b(7)
-    stage_m(1)
+    stage_c(0)
     stage_w(7)
-    stage_c(0)
     stage_c(7)
     last_parts(1)
     last_parts(2)
+    stage_m(1)
     stage_m(2)
     stage_m(0)
     stage_m(3)

time: 199 us -> 200 us (level)
  no operation moved by 1% of the time
where the time goes in v5:
time: 200 us
  Pallas kernels  197 us (98%)
  local copies, waits for them, and re-layouts  2.85 us (1%)
    pallas_call x1, Pallas kernels, shards(): pl.pallas_call(functools.partial(kernel, tok_rows, quarter, ff, cap), nam...  197 us

profile of v5, /device:TPU:1, one launch (start us, length us, event | category | flops | bytes accessed | tf_op | source)
XLA Modules:
  0.0 199.6 jit_solution(17029518540885941885)
XLA Ops:
  0.0 196.7 %routed_experts.1 = bf16[128,7168]{1,0:T(8,128)(2,1)} custom-call(s32[2,128]{1,0:T(2,128)} %bitcast.2, f32[2,128]{1,0:T(2,128)} %bitcast.3, bf16[128,7168]{1,0:T(8,128)(2,1)} %tok_ref.1, bf16[1,1792,1024]{2,1,0:T(8,128)(2,1)} %wg_ref.1, bf16[1,1792,1024]{2,1,0:T(8,128)(2,1)} %wu_ref.1, bf16[1,1024,1792]{2,1,0:T(8,128)(2,1)} %wd_ref.1), custom_call_target="tpu_custom_call" | custom-call | flops 20000000000 | bytes 15000000 | tf_op jit(solution)/shard_map/routed_experts/pallas_call | solution.py:405
  196.7 2.8 %copy.8 = bf16[128,7168]{1,0:T(8,128)(2,1)} copy(bf16[128,7168]{1,0:T(8,128)(2,1)} %routed_experts.1) | data formatting | bytes 3670016
